TPU v7x, 128 devices: a whole 4x4x4 slice. The times are simulated.
128 devices in a mesh: scen: 2 (over x_hi), hour: 16 (over z, y), reg: 4 (over x_lo, core).
Axes of the slice: x: 4 (x_hi: 2, x_lo: 2; x = x_hi * 2 + x_lo), y: 4, z: 4, core: 2. Of those that a mesh axis runs over, the one named last changes fastest.
Arguments:
- cost_rate: float32 [8, 2688, 2048], P('scen', 'hour', 'reg'), may hold values from 0.05 to 1
- invest_cost: float32 [3, 2048], P(None, 'reg'), may hold values from 0.1 to 1
- tile: bfloat16 [16, 256, 2048], P('hour', None, 'reg'), may hold values from -0.1875 to 0.1875
- tile_mask: int32 [16, 256, 2048], P('hour', None, 'reg'), may hold values 0 or 1
- demand: float32 [8, 2688, 256], P('scen', 'hour'), may hold values from -6 to 6
- dispatch: float32 [8, 2688, 2048], P('scen', 'hour', 'reg'), may hold values from 0 to 1
- dual: float32 [8, 2688, 256], P('scen', 'hour'), may hold values from 0 to 1
- cap_dual: float32 [8, 2688, 2048], P('scen', 'hour', 'reg'), may hold values from 0 to 1
- capacity: float32 [8, 3, 2048], P('scen', None, 'reg'), may hold values from 0 to 2
- multiplier: float32 [8, 3, 2048], P('scen', None, 'reg'), may hold values from -3 to 3
- consensus: float32 [8, 3, 2048], P('scen', None, 'reg'), may hold values from 0 to 2
- scen_weight: float32 [8], P('scen'), may hold values from 0.1 to 1
- node_of: int32 [3, 8], P(None, 'scen'), may hold values from 0 to 3, as said below
Outputs:
- dispatch_out: float32 [8, 2688, 2048], P('scen', 'hour', 'reg')
- dual_out: float32 [8, 2688, 256], P('scen', 'hour', 'reg')
- capacity_out: float32 [8, 3, 2048], P('scen', None, 'reg')
- multiplier_out: float32 [8, 3, 2048], P('scen', None, 'reg')
Inputs may be any that keep to these rules, and one draw needn't show every extreme that they name: `node_of`: at each section the nodes are runs of consecutive scenarios, numbered in order from 0; each node of a section lies within one node of the section before; section 0 is one node, the last section has 4 nodes, and node counts grow from section to section.
All inputs are finite; a program needn't handle non-finite values. No bound on the sum of `tile_mask` on one device may be relied on, other than what follows from the above.
Results may differ from a plain program's by a relative error of at most 0.0015.
Values may be sent and summed in bfloat16 or wider, within the bound.
A program may use at most 64 MiB of HBM per device.

v0:
```python
import jax
import jax.numpy as jnp
from jax import lax
from jax.sharding import PartitionSpec as P

ITERS = 8
RAMP_WEIGHT = 0.5
PENALTY = 1.0
STEP_PRIMAL = 0.3
STEP_INVEST = 0.5
STEP_DUAL = 0.3
STEP_CAP = 0.05


def with_halo(cells, sides, width):
    for axis, dim in sides:
        count = lax.axis_size(axis)
        ends = count - 1
        head = lax.slice_in_dim(cells, 0, width, axis=dim)
        tail = lax.slice_in_dim(cells, cells.shape[dim] - width, cells.shape[dim], axis=dim)
        cells = jnp.concatenate(
            [
                lax.ppermute(tail, axis, [(i, (i + 1) % count) for i in range(ends)]),
                cells,
                lax.ppermute(head, axis, [((i + 1) % count, i) for i in range(ends)]),
            ],
            axis=dim,
        )
    return cells


def safe_average(node_sum, node_mass):
    safe_mass = node_mass + (node_mass <= 0.0).astype(jnp.float32)
    return node_sum / safe_mass[:, :, None]


def shards(
    cost_rate,
    invest_cost,
    tile,
    tile_mask,
    demand,
    dispatch,
    dual,
    cap_dual,
    capacity,
    multiplier,
    consensus,
    scen_weight,
    node_of,
):
    matrix = tile[0] * tile_mask[0].astype(jnp.bfloat16)
    hours_all = dispatch.shape[1] * lax.axis_size("hour")
    reg_count = lax.axis_size("reg")
    reg_place = lax.axis_index("reg")
    cons_part = dual.shape[2] // reg_count
    first_row = reg_place * cons_part
    primal = dispatch
    cap_var = cap_dual
    invest = capacity
    dual_low = dual.astype(jnp.bfloat16)
    dual_var = dual
    for step_index in range(ITERS):
        padded = with_halo(primal, (("hour", 1),), 1)
        rough = 2.0 * primal - padded[:, :-2] - padded[:, 2:]
        pulled = jnp.einsum("shr,rc->shc", dual_low, matrix, preferred_element_type=jnp.float32)
        grad_x = cost_rate + RAMP_WEIGHT * rough - pulled + cap_var
        zmean = lax.psum(jnp.sum(cap_var, axis=1), "hour") / hours_all
        grad_u = invest_cost[None] + multiplier + PENALTY * (invest - consensus) - zmean[:, None, :]
        primal_new = jnp.maximum(primal - STEP_PRIMAL * grad_x, 0.0)
        invest_new = jnp.maximum(invest - STEP_INVEST * grad_u, 0.0)
        primal_ext = 2.0 * primal_new - primal
        invest_ext = 2.0 * invest_new - invest
        partial_rows = jnp.einsum(
            "shc,rc->shr",
            primal_ext.astype(jnp.bfloat16),
            matrix,
            preferred_element_type=jnp.float32,
        )
        image = lax.psum(partial_rows, "reg")
        dual_var = jnp.maximum(dual_var + STEP_DUAL * (demand - image), 0.0)
        dual_low = dual_var.astype(jnp.bfloat16)
        cap_var = jnp.maximum(
            cap_var + STEP_CAP * (primal_ext - jnp.sum(invest_ext, axis=1)[:, None, :]), 0.0
        )
        primal = primal_new
        invest = invest_new
    dual_out = lax.dynamic_slice_in_dim(dual_var, first_row, cons_part, 2)
    node_count = node_of.shape[1] * lax.axis_size("scen") // 2
    node_ids = jnp.arange(node_count, dtype=jnp.int32)
    one_hot = (node_of[:, :, None] == node_ids[None, None, :]).astype(jnp.float32)
    weighted = scen_weight[:, None, None] * invest
    node_sum = jnp.einsum("gsn,sgc->gnc", one_hot, weighted, precision=lax.Precision.HIGHEST)
    node_mass = jnp.einsum("gsn,s->gn", one_hot, scen_weight, precision=lax.Precision.HIGHEST)
    sum_total, mass_total = lax.psum((node_sum, node_mass), "scen")
    average = safe_average(sum_total, mass_total)
    spread_back = jnp.einsum("gsn,gnc->sgc", one_hot, average, precision=lax.Precision.HIGHEST)
    multiplier_out = multiplier + PENALTY * (invest - spread_back)
    return (primal, dual_out, invest, multiplier_out)


def solution(mesh):
    placed = (
        P("scen", "hour", "reg"),
        P(None, "reg"),
        P("hour", None, "reg"),
        P("hour", None, "reg"),
        P("scen", "hour", None),
        P("scen", "hour", "reg"),
        P("scen", "hour", None),
        P("scen", "hour", "reg"),
        P("scen", None, "reg"),
        P("scen", None, "reg"),
        P("scen", None, "reg"),
        P("scen"),
        P(None, "scen"),
    )
    return jax.shard_map(
        shards,
        mesh=mesh,
        in_specs=placed,
        out_specs=(
            P("scen", "hour", "reg"),
            P("scen", "hour", "reg"),
            P("scen", None, "reg"),
            P("scen", None, "reg"),
        ),
        check_vma=False,
    )
```

profile of v0, /device:TPU:1, one launch (start us, length us, event | category | flops | bytes accessed | tf_op | source)
XLA Modules:
  0.0 458.1 jit_solution(8639232075780562060)
XLA Ops:
  8.3 4.0 collective-permute-start
  15.1 36.1 %psum.127 = f32[4,512]{1,0:T(4,128)S(1)} all-reduce(f32[4,512]{1,0:T(4,128)S(1)} %reduce_sum.135), channel_id=1, replica_groups=mesh['scen'=2,'hour'=16,'reg'=4] {'hour'}, use_global_device_ids=true, to_apply=%region_2.0 | all-reduce | flops 2048 | bytes 16384 | tf_op jit(solution)/shard_map/psum | solution.py:68
  52.5 5.1 %fusion.169 = (f32[4,512]{1,0:T(4,128)S(1)}, f32[4,168,512]{2,1,0:T(8,128)}, f32[4,168,512]{2,1,0:T(8,128)S(1)}) fusion(f32[4,168,512]{2,1,0:T(8,128)} %param.20, f32[4,512]{1,0:T(4,128)S(1)} %get-tuple-element.22, f32[4,168,512]{2,1,0:T(8,128)} %param.18, f32[4,168,256]{2,1,0:T(8,128)S(1)} %copy-done.20, ...), kind=kOutput, calls=%fused_computation.223 | convolution fusion | flops 182867968 | bytes 7864320 | tf_op jit(solution)/shard_map/shr,rc->shc/dot_general | solution.py:66
  63.6 31.5 %psum.129 = f32[4,512]{1,0:T(4,128)S(1)} all-reduce(f32[4,512]{1,0:T(4,128)S(1)} %get-tuple-element.20), channel_id=1, replica_groups=mesh['scen'=2,'hour'=16,'reg'=4] {'hour'}, use_global_device_ids=true, to_apply=%region_6.0 | all-reduce | flops 2048 | bytes 16384 | tf_op jit(solution)/shard_map/psum | solution.py:68
  95.1 8.0 %all-reduce.10.cloned.1.call-done = f32[4,168,256]{2,1,0:T(8,128)} async-done(((f32[4,168,256]{2,1,0:T(8,128)}), f32[4,168,256]{2,1,0:T(8,128)}) %all-reduce.10.cloned.1.call-update) | async-done | bytes 688144 | tf_op jit(solution)/shard_map/psum | solution.py:80
  103.2 5.2 %fusion.168 = (f32[4,512]{1,0:T(4,128)S(1)}, f32[4,168,512]{2,1,0:T(8,128)}, f32[4,168,512]{2,1,0:T(8,128)S(1)}) fusion(f32[4,168,512]{2,1,0:T(8,128)} %get-tuple-element.21, f32[4,512]{1,0:T(4,128)S(1)} %subtract_reduce_fusion.5, f32[4,168,512]{2,1,0:T(8,128)} %copy-done.11, bf16[1,256,512]{2,1,0:T(8,128)(2,1)S(1)} %convert_multiply_fusion, ...), kind=kOutput, calls=%fused_computation.222 | convolution fusion | flops 183556096 | bytes 9240576 | tf_op jit(solution)/shard_map/shr,rc->shc/dot_general | solution.py:66
  111.7 3.1 collective-permute-start.4
  116.1 35.6 %psum.131 = f32[4,512]{1,0:T(4,128)S(1)} all-reduce(f32[4,512]{1,0:T(4,128)S(1)} %get-tuple-element.18), channel_id=1, replica_groups=mesh['scen'=2,'hour'=16,'reg'=4] {'hour'}, use_global_device_ids=true, to_apply=%region_10.0 | all-reduce | flops 2048 | bytes 16384 | tf_op jit(solution)/shard_map/psum | solution.py:68
  161.3 3.1 collective-permute-start.6
  165.7 36.0 %psum.133 = f32[4,512]{1,0:T(4,128)S(1)} all-reduce(f32[4,512]{1,0:T(4,128)S(1)} %get-tuple-element.16), channel_id=1, replica_groups=mesh['scen'=2,'hour'=16,'reg'=4] {'hour'}, use_global_device_ids=true, to_apply=%region_14.0 | all-reduce | flops 2048 | bytes 16384 | tf_op jit(solution)/shard_map/psum | solution.py:68
  202.9 5.2 %fusion.166 = (f32[4,512]{1,0:T(4,128)S(1)}, f32[4,168,512]{2,1,0:T(8,128)}, f32[4,168,512]{2,1,0:T(8,128)S(1)}) fusion(f32[4,168,512]{2,1,0:T(8,128)} %get-tuple-element.17, f32[4,512]{1,0:T(4,128)S(1)} %subtract_reduce_fusion.3, f32[4,168,512]{2,1,0:T(8,128)} %copy-done.7, bf16[1,256,512]{2,1,0:T(8,128)(2,1)S(1)} %convert_multiply_fusion, ...), kind=kOutput, calls=%fused_computation.220 | convolution fusion | flops 183556096 | bytes 9240576 | tf_op jit(solution)/shard_map/shr,rc->shc/dot_general | solution.py:66
  211.5 3.1 collective-permute-start.8
  215.8 35.3 %psum.135 = f32[4,512]{1,0:T(4,128)S(1)} all-reduce(f32[4,512]{1,0:T(4,128)S(1)} %get-tuple-element.14), channel_id=1, replica_groups=mesh['scen'=2,'hour'=16,'reg'=4] {'hour'}, use_global_device_ids=true, to_apply=%region_18.0 | all-reduce | flops 2048 | bytes 16384 | tf_op jit(solution)/shard_map/psum | solution.py:68
  260.9 3.1 collective-permute-start.10
  265.2 35.5 %psum.137 = f32[4,512]{1,0:T(4,128)S(1)} all-reduce(f32[4,512]{1,0:T(4,128)S(1)} %get-tuple-element.12), channel_id=1, replica_groups=mesh['scen'=2,'hour'=16,'reg'=4] {'hour'}, use_global_device_ids=true, to_apply=%region_22.0 | all-reduce | flops 2048 | bytes 16384 | tf_op jit(solution)/shard_map/psum | solution.py:68
  302.8 5.5 %fusion.164 = (f32[4,512]{1,0:T(4,128)S(1)}, f32[4,168,512]{2,1,0:T(8,128)}, f32[4,168,512]{2,1,0:T(8,128)S(1)}) fusion(f32[4,168,512]{2,1,0:T(8,128)} %get-tuple-element.13, f32[4,512]{1,0:T(4,128)S(1)} %subtract_reduce_fusion.1, f32[4,168,512]{2,1,0:T(8,128)} %copy-done.9, bf16[1,256,512]{2,1,0:T(8,128)(2,1)S(1)} %convert_multiply_fusion, ...), kind=kOutput, calls=%fused_computation.218 | convolution fusion | flops 183556096 | bytes 9240576 | tf_op jit(solution)/shard_map/shr,rc->shc/dot_general | solution.py:66
  309.7 3.1 collective-permute-start.12
  314.1 35.3 %psum.139 = f32[4,512]{1,0:T(4,128)S(1)} all-reduce(f32[4,512]{1,0:T(4,128)S(1)} %get-tuple-element.10), channel_id=1, replica_groups=mesh['scen'=2,'hour'=16,'reg'=4] {'hour'}, use_global_device_ids=true, to_apply=%region_26.0 | all-reduce | flops 2048 | bytes 16384 | tf_op jit(solution)/shard_map/psum | solution.py:68
  349.6 2.7 all-reduce.20.cloned.1.call-done
  352.3 3.4 fusion.139
  359.2 3.2 collective-permute-start.14
  363.8 35.2 %psum.141 = f32[4,512]{1,0:T(4,128)S(1)} all-reduce(f32[4,512]{1,0:T(4,128)S(1)} %get-tuple-element.46), channel_id=1, replica_groups=mesh['scen'=2,'hour'=16,'reg'=4] {'hour'}, use_global_device_ids=true, to_apply=%region_30.0 | all-reduce | flops 2048 | bytes 16384 | tf_op jit(solution)/shard_map/psum | solution.py:68
  406.4 9.4 %all-reduce = (f32[3,4,512]{2,1,0:T(4,128)S(1)}, f32[3,4]{1,0:T(4,128)S(1)}) all-reduce(f32[3,4,512]{2,1,0:T(4,128)S(1)} %fusion.140, f32[3,4]{1,0:T(4,128)S(1)} %bitcast.64), channel_id=1, replica_groups=mesh['scen'=2,'hour'=16,'reg'=4] {'scen'}, use_global_device_ids=true, to_apply=%region_31.0 | all-reduce | flops 6156 | bytes 49248 | tf_op jit(solution)/shard_map/psum | solution.py:95
  416.7 32.3 %all-reduce.24.cloned.1.call-done = f32[4,168,256]{2,1,0:T(8,128)} async-done(((f32[4,168,256]{2,1,0:T(8,128)}), f32[4,168,256]{2,1,0:T(8,128)}) %all-reduce.24.cloned.1.call-update) | async-done | bytes 688144 | tf_op jit(solution)/shard_map/psum | solution.py:80
  (157 shorter events, 63.2 us)
Async XLA Ops:
  7.2 95.9 %all-reduce.10.cloned.1.call-start = ((), (), s32[]{:S(2)}) async-start(), calls=%async_computation | async-start | bytes 1376256 | tf_op jit(solution)/shard_map/psum | solution.py:80
  8.3 44.1 %collective-permute-start = (f32[4,1,512]{2,1,0:T(1,128)S(1)}, f32[4,1,512]{2,1,0:T(1,128)S(1)}, u32[]{:S(2)}, u32[]{:S(2)}) collective-permute-start(f32[4,1,512]{2,1,0:T(1,128)S(1)} %get-tuple-element.38), channel_id=1, source_target_pairs={{0,4},{4,8},{8,12},{12,16},{16,20},{20,24},{24,28},{28,32},{32,36}... | collective-permute-start | bytes 24584 | tf_op jit(solution)/shard_map/ppermute | solution.py:23
  12.4 40.1 %collective-permute-start.1 = (f32[4,1,512]{2,1,0:T(1,128)S(1)}, f32[4,1,512]{2,1,0:T(1,128)S(1)}, u32[]{:S(2)}, u32[]{:S(2)}) collective-permute-start(f32[4,1,512]{2,1,0:T(1,128)S(1)} %get-tuple-element.39), channel_id=1, source_target_pairs={{4,0},{8,4},{12,8},{16,12},{20,16},{24,20},{28,24},{32,28},{36,32}... | collective-permute-start | bytes 24584 | tf_op jit(solution)/shard_map/ppermute | solution.py:25
  60.0 93.4 %all-reduce.12.cloned.1.call-start = ((), (), s32[]{:S(2)}) async-start(), calls=%async_computation.1 | async-start | bytes 1376256 | tf_op jit(solution)/shard_map/psum | solution.py:80
  61.0 34.1 %collective-permute-start.2 = (f32[4,1,512]{2,1,0:T(1,128)S(1)}, f32[4,1,512]{2,1,0:T(1,128)S(1)}, u32[]{:S(2)}, u32[]{:S(2)}) collective-permute-start(f32[4,1,512]{2,1,0:T(1,128)S(1)} %get-tuple-element.36), channel_id=1, source_target_pairs={{0,4},{4,8},{8,12},{12,16},{16,20},{20,24},{24,28},{28,32},{32,36}... | collective-permute-start | bytes 24584 | tf_op jit(solution)/shard_map/ppermute | solution.py:23
  62.3 32.8 %collective-permute-start.3 = (f32[4,1,512]{2,1,0:T(1,128)S(1)}, f32[4,1,512]{2,1,0:T(1,128)S(1)}, u32[]{:S(2)}, u32[]{:S(2)}) collective-permute-start(f32[4,1,512]{2,1,0:T(1,128)S(1)} %get-tuple-element.37), channel_id=1, source_target_pairs={{4,0},{8,4},{12,8},{16,12},{20,16},{24,20},{28,24},{32,28},{36,32}... | collective-permute-start | bytes 24584 | tf_op jit(solution)/shard_map/ppermute | solution.py:25
  110.8 92.1 %all-reduce.14.cloned.1.call-start = ((), (), s32[]{:S(2)}) async-start(), calls=%async_computation.2 | async-start | bytes 1376256 | tf_op jit(solution)/shard_map/psum | solution.py:80
  111.7 43.5 %collective-permute-start.4 = (f32[4,1,512]{2,1,0:T(1,128)S(1)}, f32[4,1,512]{2,1,0:T(1,128)S(1)}, u32[]{:S(2)}, u32[]{:S(2)}) collective-permute-start(f32[4,1,512]{2,1,0:T(1,128)S(1)} %get-tuple-element.34), channel_id=1, source_target_pairs={{0,4},{4,8},{8,12},{12,16},{16,20},{20,24},{24,28},{28,32},{32,36}... | collective-permute-start | bytes 24584 | tf_op jit(solution)/shard_map/ppermute | solution.py:23
  114.8 40.5 %collective-permute-start.5 = (f32[4,1,512]{2,1,0:T(1,128)S(1)}, f32[4,1,512]{2,1,0:T(1,128)S(1)}, u32[]{:S(2)}, u32[]{:S(2)}) collective-permute-start(f32[4,1,512]{2,1,0:T(1,128)S(1)} %get-tuple-element.35), channel_id=1, source_target_pairs={{4,0},{8,4},{12,8},{16,12},{20,16},{24,20},{28,24},{32,28},{36,32}... | collective-permute-start | bytes 24584 | tf_op jit(solution)/shard_map/ppermute | solution.py:25
  160.4 92.8 %all-reduce.16.cloned.1.call-start = ((), (), s32[]{:S(2)}) async-start(), calls=%async_computation.3 | async-start | bytes 1376256 | tf_op jit(solution)/shard_map/psum | solution.py:80
  161.3 40.5 %collective-permute-start.6 = (f32[4,1,512]{2,1,0:T(1,128)S(1)}, f32[4,1,512]{2,1,0:T(1,128)S(1)}, u32[]{:S(2)}, u32[]{:S(2)}) collective-permute-start(f32[4,1,512]{2,1,0:T(1,128)S(1)} %get-tuple-element.32), channel_id=1, source_target_pairs={{0,4},{4,8},{8,12},{12,16},{16,20},{20,24},{24,28},{28,32},{32,36}... | collective-permute-start | bytes 24584 | tf_op jit(solution)/shard_map/ppermute | solution.py:23
  164.4 37.4 %collective-permute-start.7 = (f32[4,1,512]{2,1,0:T(1,128)S(1)}, f32[4,1,512]{2,1,0:T(1,128)S(1)}, u32[]{:S(2)}, u32[]{:S(2)}) collective-permute-start(f32[4,1,512]{2,1,0:T(1,128)S(1)} %get-tuple-element.33), channel_id=1, source_target_pairs={{4,0},{8,4},{12,8},{16,12},{20,16},{24,20},{28,24},{32,28},{36,32}... | collective-permute-start | bytes 24584 | tf_op jit(solution)/shard_map/ppermute | solution.py:25
  210.5 92.2 %all-reduce.18.cloned.1.call-start = ((), (), s32[]{:S(2)}) async-start(), calls=%async_computation.4 | async-start | bytes 1376256 | tf_op jit(solution)/shard_map/psum | solution.py:80
  211.5 43.4 %collective-permute-start.8 = (f32[4,1,512]{2,1,0:T(1,128)S(1)}, f32[4,1,512]{2,1,0:T(1,128)S(1)}, u32[]{:S(2)}, u32[]{:S(2)}) collective-permute-start(f32[4,1,512]{2,1,0:T(1,128)S(1)} %get-tuple-element.30), channel_id=1, source_target_pairs={{0,4},{4,8},{8,12},{12,16},{16,20},{20,24},{24,28},{28,32},{32,36}... | collective-permute-start | bytes 24584 | tf_op jit(solution)/shard_map/ppermute | solution.py:23
  214.5 40.3 %collective-permute-start.9 = (f32[4,1,512]{2,1,0:T(1,128)S(1)}, f32[4,1,512]{2,1,0:T(1,128)S(1)}, u32[]{:S(2)}, u32[]{:S(2)}) collective-permute-start(f32[4,1,512]{2,1,0:T(1,128)S(1)} %get-tuple-element.31), channel_id=1, source_target_pairs={{4,0},{8,4},{12,8},{16,12},{20,16},{24,20},{28,24},{32,28},{36,32}... | collective-permute-start | bytes 24584 | tf_op jit(solution)/shard_map/ppermute | solution.py:25
  259.9 92.4 %all-reduce.20.cloned.1.call-start = ((), (), s32[]{:S(2)}) async-start(), calls=%async_computation.5 | async-start | bytes 1376256 | tf_op jit(solution)/shard_map/psum | solution.py:80
  260.9 40.0 %collective-permute-start.10 = (f32[4,1,512]{2,1,0:T(1,128)S(1)}, f32[4,1,512]{2,1,0:T(1,128)S(1)}, u32[]{:S(2)}, u32[]{:S(2)}) collective-permute-start(f32[4,1,512]{2,1,0:T(1,128)S(1)} %get-tuple-element.28), channel_id=1, source_target_pairs={{0,4},{4,8},{8,12},{12,16},{16,20},{20,24},{24,28},{28,32},{32,36}... | collective-permute-start | bytes 24584 | tf_op jit(solution)/shard_map/ppermute | solution.py:23
  263.9 36.9 %collective-permute-start.11 = (f32[4,1,512]{2,1,0:T(1,128)S(1)}, f32[4,1,512]{2,1,0:T(1,128)S(1)}, u32[]{:S(2)}, u32[]{:S(2)}) collective-permute-start(f32[4,1,512]{2,1,0:T(1,128)S(1)} %get-tuple-element.29), channel_id=1, source_target_pairs={{4,0},{8,4},{12,8},{16,12},{20,16},{24,20},{28,24},{32,28},{36,32}... | collective-permute-start | bytes 24584 | tf_op jit(solution)/shard_map/ppermute | solution.py:25
  309.6 90.3 %all-reduce.22.cloned.1.call-start = ((), (), s32[]{:S(2)}) async-start(), calls=%async_computation.6 | async-start | bytes 1376256 | tf_op jit(solution)/shard_map/psum | solution.py:80
  309.7 39.8 %collective-permute-start.12 = (f32[4,1,512]{2,1,0:T(1,128)S(1)}, f32[4,1,512]{2,1,0:T(1,128)S(1)}, u32[]{:S(2)}, u32[]{:S(2)}) collective-permute-start(f32[4,1,512]{2,1,0:T(1,128)S(1)} %get-tuple-element.26), channel_id=1, source_target_pairs={{0,4},{4,8},{8,12},{12,16},{16,20},{20,24},{24,28},{28,32},{32,36}... | collective-permute-start | bytes 24584 | tf_op jit(solution)/shard_map/ppermute | solution.py:23
  312.8 36.8 %collective-permute-start.13 = (f32[4,1,512]{2,1,0:T(1,128)S(1)}, f32[4,1,512]{2,1,0:T(1,128)S(1)}, u32[]{:S(2)}, u32[]{:S(2)}) collective-permute-start(f32[4,1,512]{2,1,0:T(1,128)S(1)} %get-tuple-element.27), channel_id=1, source_target_pairs={{4,0},{8,4},{12,8},{16,12},{20,16},{24,20},{28,24},{32,28},{36,32}... | collective-permute-start | bytes 24584 | tf_op jit(solution)/shard_map/ppermute | solution.py:25
  358.1 90.9 %all-reduce.24.cloned.1.call-start = ((), (), s32[]{:S(2)}) async-start(), calls=%async_computation.7 | async-start | bytes 1376256 | tf_op jit(solution)/shard_map/psum | solution.py:80
  359.2 42.7 %collective-permute-start.14 = (f32[4,1,512]{2,1,0:T(1,128)S(1)}, f32[4,1,512]{2,1,0:T(1,128)S(1)}, u32[]{:S(2)}, u32[]{:S(2)}) collective-permute-start(f32[4,1,512]{2,1,0:T(1,128)S(1)} %get-tuple-element.24), channel_id=1, source_target_pairs={{0,4},{4,8},{8,12},{12,16},{16,20},{20,24},{24,28},{28,32},{32,36}... | collective-permute-start | bytes 24584 | tf_op jit(solution)/shard_map/ppermute | solution.py:23
  362.5 39.4 %collective-permute-start.15 = (f32[4,1,512]{2,1,0:T(1,128)S(1)}, f32[4,1,512]{2,1,0:T(1,128)S(1)}, u32[]{:S(2)}, u32[]{:S(2)}) collective-permute-start(f32[4,1,512]{2,1,0:T(1,128)S(1)} %get-tuple-element.25), channel_id=1, source_target_pairs={{4,0},{8,4},{12,8},{16,12},{20,16},{24,20},{28,24},{32,28},{36,32}... | collective-permute-start | bytes 24584 | tf_op jit(solution)/shard_map/ppermute | solution.py:25
  (32 other events, 475.4 us)
Sparse Core Ops, SparseCore 0:
  60.2 42.9 all-reduce.9
  110.9 42.4 all-reduce.11
  160.5 42.3 all-reduce.13
  210.6 42.4 all-reduce.15
  260.0 42.6 all-reduce.17
  309.7 42.4 all-reduce.19
  358.2 41.6 all-reduce.21
  406.3 42.6 all-reduce.23
where the time goes:
time: 459 us; the launch traced here: 458 us
  blocking collectives  290 us (63%)
  waiting for transfers between devices  50.6 us (11%)
  matrix products  41.5 us (9%)
  starting transfers between devices  34.5 us (8%)
  local copies, waits for them, and re-layouts  16.7 us (4%)
  between operations  14.8 us (3%)
  other arithmetic  10.1 us (2%)
    psum x8, blocking collectives, shards(): zmean = lax.psum(jnp.sum(cap_var, axis=1), 'hour') / hours_all  281 us
    psum x8, waiting for transfers between devices, shards(): image = lax.psum(partial_rows, 'reg')  50.4 us
    dot_general x8, matrix products, shards(): jnp.einsum('shr,rc->shc', dual_low, matrix, preferred_element_type=jnp.fl...  30 us
    ppermute x8, starting transfers between devices, with_halo(): lax.ppermute(tail, axis, [(i, (i + 1) % count) for i in range(ends)])  23.9 us
    unnamed x65, local copies, waits for them, and re-layouts  10.4 us
    ppermute x8, starting transfers between devices, with_halo(): lax.ppermute(head, axis, [((i + 1) % count, i) for i in range(ends)])  10.3 us
    dot_general x8, matrix products, shards(): jnp.einsum('shc,rc->shr', primal_ext.astype(jnp.bfloat16), matrix, prefer...  10.2 us
    psum x1, blocking collectives, shards(): sum_total, mass_total = lax.psum((node_sum, node_mass), 'scen')  9.39 us
  transfers between devices with their start and end apart: 24, of which 8 were waited for; matrix products, arithmetic and copies ran while one was open for 3% of the time, Pallas kernels for 0%

commit v1 on v0

--- a/solution.py
+++ b/solution.py
@@ -77,7 +77,8 @@
             matrix,
             preferred_element_type=jnp.float32,
         )
-        image = lax.psum(partial_rows, "reg")
+        shards_2 = lax.all_gather(partial_rows, "reg")
+        image = jnp.sum(shards_2, axis=0)
         dual_var = jnp.maximum(dual_var + STEP_DUAL * (demand - image), 0.0)
         dual_low = dual_var.astype(jnp.bfloat16)
         cap_var = jnp.maximum(

time: 459 us -> 485 us (1.057); the launches traced: 458 us -> 476 us
  other arithmetic: 10.1 us -> 30.7 us
  blocking collectives: 290 us -> 285 us
    all_gather x0 -> x8, waiting for transfers between devices: none -> 53.2 us  [shards(): shards_2 = lax.all_gather(partial_rows, 'reg')]
    psum x8 -> x0, waiting for transfers between devices: 50.4 us -> none  [shards(): image = lax.psum(partial_rows, 'reg')]
    reduce_sum x0 -> x8, other arithmetic: none -> 21.7 us  [shards(): image = jnp.sum(shards_2, axis=0)]
    psum x8, blocking collectives: 281 us -> 275 us  [shards(): zmean = lax.psum(jnp.sum(cap_var, axis=1), 'hour') / hours_all]
    unnamed x65 -> x69, local copies, waits for them, and re-layouts: 10.4 us -> 10.3 us
  transfers between devices with their start and end apart: 24 -> 24, of which waited for: 8 -> 7; matrix products, arithmetic and copies ran while one was open for 3% -> 7% of each run, Pallas kernels for 0% -> 0%
where the time goes in v1:
time: 485 us; the launch traced here: 476 us
  blocking collectives  285 us (59%)
  waiting for transfers between devices  53.3 us (11%)
  matrix products  41.3 us (9%)
  starting transfers between devices  34.7 us (7%)
  other arithmetic  30.7 us (6%)
  local copies, waits for them, and re-layouts  16.6 us (3%)
  between operations  14.8 us (3%)
    psum x8, blocking collectives, shards(): zmean = lax.psum(jnp.sum(cap_var, axis=1), 'hour') / hours_all  275 us
    all_gather x8, waiting for transfers between devices, shards(): shards_2 = lax.all_gather(partial_rows, 'reg')  53.2 us
    dot_general x8, matrix products, shards(): jnp.einsum('shr,rc->shc', dual_low, matrix, preferred_element_type=jnp.fl...  29.8 us
    ppermute x8, starting transfers between devices, with_halo(): lax.ppermute(tail, axis, [(i, (i + 1) % count) for i in range(ends)])  24 us
    reduce_sum x8, other arithmetic, shards(): image = jnp.sum(shards_2, axis=0)  21.7 us
    ppermute x8, starting transfers between devices, with_halo(): lax.ppermute(head, axis, [((i + 1) % count, i) for i in range(ends)])  10.3 us
    unnamed x69, local copies, waits for them, and re-layouts  10.3 us
    dot_general x8, matrix products, shards(): jnp.einsum('shc,rc->shr', primal_ext.astype(jnp.bfloat16), matrix, prefer...  10.2 us
  transfers between devices with their start and end apart: 24, of which 7 were waited for; matrix products, arithmetic and copies ran while one was open for 7% of the time, Pallas kernels for 0%

profile of v1, /device:TPU:1, one launch (start us, length us, event | category | flops | bytes accessed | tf_op | source)
XLA Modules:
  0.0 476.3 jit_solution(18385368294072431387)
XLA Ops:
  8.3 4.0 collective-permute-start
  15.1 36.1 %psum.70 = f32[4,512]{1,0:T(4,128)S(1)} all-reduce(f32[4,512]{1,0:T(4,128)S(1)} %reduce_sum.208), channel_id=1, replica_groups=mesh['scen'=2,'hour'=16,'reg'=4] {'hour'}, use_global_device_ids=true, to_apply=%region_2.0 | all-reduce | flops 2048 | bytes 16384 | tf_op jit(solution)/shard_map/psum | solution.py:68
  52.5 4.9 %fusion.169 = (f32[4,512]{1,0:T(4,128)S(1)}, f32[4,168,512]{2,1,0:T(8,128)}, f32[4,168,512]{2,1,0:T(8,128)S(1)}) fusion(f32[4,168,512]{2,1,0:T(8,128)} %param.20, f32[4,512]{1,0:T(4,128)S(1)} %get-tuple-element.22, f32[4,168,512]{2,1,0:T(8,128)} %param.18, f32[4,168,256]{2,1,0:T(8,128)S(1)} %copy-done.22, ...), kind=kOutput, calls=%fused_computation.223 | convolution fusion | flops 182867968 | bytes 7864320 | tf_op jit(solution)/shard_map/shr,rc->shc/dot_general | solution.py:66
  63.3 31.5 %psum.71 = f32[4,512]{1,0:T(4,128)S(1)} all-reduce(f32[4,512]{1,0:T(4,128)S(1)} %get-tuple-element.20), channel_id=1, replica_groups=mesh['scen'=2,'hour'=16,'reg'=4] {'hour'}, use_global_device_ids=true, to_apply=%region_6.0 | all-reduce | flops 2048 | bytes 16384 | tf_op jit(solution)/shard_map/psum | solution.py:68
  94.9 4.0 all-gather.17.cloned.1.call-done
  101.0 5.3 %fusion.168 = (f32[4,512]{1,0:T(4,128)S(1)}, f32[4,168,512]{2,1,0:T(8,128)}, f32[4,168,512]{2,1,0:T(8,128)S(1)}) fusion(f32[4,168,512]{2,1,0:T(8,128)} %get-tuple-element.21, f32[4,512]{1,0:T(4,128)S(1)} %subtract_reduce_fusion.5, f32[4,168,512]{2,1,0:T(8,128)} %copy-done.11, bf16[1,256,512]{2,1,0:T(8,128)(2,1)S(1)} %convert_multiply_fusion, ...), kind=kOutput, calls=%fused_computation.222 | convolution fusion | flops 183556096 | bytes 9240576 | tf_op jit(solution)/shard_map/shr,rc->shc/dot_general | solution.py:66
  109.6 3.1 collective-permute-start.4
  114.0 34.7 %psum.72 = f32[4,512]{1,0:T(4,128)S(1)} all-reduce(f32[4,512]{1,0:T(4,128)S(1)} %get-tuple-element.18), channel_id=1, replica_groups=mesh['scen'=2,'hour'=16,'reg'=4] {'hour'}, use_global_device_ids=true, to_apply=%region_10.0 | all-reduce | flops 2048 | bytes 16384 | tf_op jit(solution)/shard_map/psum | solution.py:68
  162.1 3.1 collective-permute-start.6
  166.5 34.7 %psum.73 = f32[4,512]{1,0:T(4,128)S(1)} all-reduce(f32[4,512]{1,0:T(4,128)S(1)} %get-tuple-element.16), channel_id=1, replica_groups=mesh['scen'=2,'hour'=16,'reg'=4] {'hour'}, use_global_device_ids=true, to_apply=%region_14.0 | all-reduce | flops 2048 | bytes 16384 | tf_op jit(solution)/shard_map/psum | solution.py:68
  206.7 5.2 %fusion.166 = (f32[4,512]{1,0:T(4,128)S(1)}, f32[4,168,512]{2,1,0:T(8,128)}, f32[4,168,512]{2,1,0:T(8,128)S(1)}) fusion(f32[4,168,512]{2,1,0:T(8,128)} %get-tuple-element.17, f32[4,512]{1,0:T(4,128)S(1)} %subtract_reduce_fusion.3, f32[4,168,512]{2,1,0:T(8,128)} %copy-done.7, bf16[1,256,512]{2,1,0:T(8,128)(2,1)S(1)} %convert_multiply_fusion, ...), kind=kOutput, calls=%fused_computation.220 | convolution fusion | flops 183556096 | bytes 9240576 | tf_op jit(solution)/shard_map/shr,rc->shc/dot_general | solution.py:66
  215.2 3.1 collective-permute-start.8
  219.6 34.7 %psum.74 = f32[4,512]{1,0:T(4,128)S(1)} all-reduce(f32[4,512]{1,0:T(4,128)S(1)} %get-tuple-element.14), channel_id=1, replica_groups=mesh['scen'=2,'hour'=16,'reg'=4] {'hour'}, use_global_device_ids=true, to_apply=%region_18.0 | all-reduce | flops 2048 | bytes 16384 | tf_op jit(solution)/shard_map/psum | solution.py:68
  267.4 3.1 collective-permute-start.10
  271.9 34.9 %psum.75 = f32[4,512]{1,0:T(4,128)S(1)} all-reduce(f32[4,512]{1,0:T(4,128)S(1)} %get-tuple-element.12), channel_id=1, replica_groups=mesh['scen'=2,'hour'=16,'reg'=4] {'hour'}, use_global_device_ids=true, to_apply=%region_22.0 | all-reduce | flops 2048 | bytes 16384 | tf_op jit(solution)/shard_map/psum | solution.py:68
  312.1 5.6 %fusion.164 = (f32[4,512]{1,0:T(4,128)S(1)}, f32[4,168,512]{2,1,0:T(8,128)}, f32[4,168,512]{2,1,0:T(8,128)S(1)}) fusion(f32[4,168,512]{2,1,0:T(8,128)} %get-tuple-element.13, f32[4,512]{1,0:T(4,128)S(1)} %subtract_reduce_fusion.1, f32[4,168,512]{2,1,0:T(8,128)} %copy-done.9, bf16[1,256,512]{2,1,0:T(8,128)(2,1)S(1)} %convert_multiply_fusion, ...), kind=kOutput, calls=%fused_computation.218 | convolution fusion | flops 183556096 | bytes 9240576 | tf_op jit(solution)/shard_map/shr,rc->shc/dot_general | solution.py:66
  319.1 3.1 collective-permute-start.12
  323.5 34.9 %psum.76 = f32[4,512]{1,0:T(4,128)S(1)} all-reduce(f32[4,512]{1,0:T(4,128)S(1)} %get-tuple-element.10), channel_id=1, replica_groups=mesh['scen'=2,'hour'=16,'reg'=4] {'hour'}, use_global_device_ids=true, to_apply=%region_26.0 | all-reduce | flops 2048 | bytes 16384 | tf_op jit(solution)/shard_map/psum | solution.py:68
  358.5 3.3 all-gather.27.cloned.1.call-done
  364.7 3.4 fusion.139
  371.5 3.1 collective-permute-start.14
  375.9 36.4 %all-gather.29.cloned.1.call-done = f32[16,168,256]{2,1,0:T(8,128)} async-done(((f32[4,168,256]{2,1,0:T(8,128)}), f32[16,168,256]{2,1,0:T(8,128)}) %all-gather.29.cloned.1.call-update) | async-done | bytes 2752528 | tf_op jit(solution)/shard_map/all_gather | solution.py:80
  421.7 33.8 %psum.77 = f32[4,512]{1,0:T(4,128)S(1)} all-reduce(f32[4,512]{1,0:T(4,128)S(1)} %get-tuple-element.46), channel_id=1, replica_groups=mesh['scen'=2,'hour'=16,'reg'=4] {'hour'}, use_global_device_ids=true, to_apply=%region_30.0 | all-reduce | flops 2048 | bytes 16384 | tf_op jit(solution)/shard_map/psum | solution.py:68
  455.9 9.3 %all-reduce = (f32[3,4,512]{2,1,0:T(4,128)S(1)}, f32[3,4]{1,0:T(4,128)S(1)}) all-reduce(f32[3,4,512]{2,1,0:T(4,128)S(1)} %fusion.140, f32[3,4]{1,0:T(4,128)S(1)} %bitcast.80), channel_id=1, replica_groups=mesh['scen'=2,'hour'=16,'reg'=4] {'scen'}, use_global_device_ids=true, to_apply=%region_31.0 | all-reduce | flops 6156 | bytes 49248 | tf_op jit(solution)/shard_map/psum | solution.py:96
  (169 shorter events, 85.9 us)
Async XLA Ops:
  7.2 91.6 %all-gather.17.cloned.1.call-start = ((), (), s32[]{:S(2)}) async-start(), calls=%async_computation | async-start | bytes 3440640 | tf_op jit(solution)/shard_map/all_gather | solution.py:80
  8.3 44.1 %collective-permute-start = (f32[4,1,512]{2,1,0:T(1,128)S(1)}, f32[4,1,512]{2,1,0:T(1,128)S(1)}, u32[]{:S(2)}, u32[]{:S(2)}) collective-permute-start(f32[4,1,512]{2,1,0:T(1,128)S(1)} %get-tuple-element.38), channel_id=1, source_target_pairs={{0,4},{4,8},{8,12},{12,16},{16,20},{20,24},{24,28},{28,32},{32,36}... | collective-permute-start | bytes 24584 | tf_op jit(solution)/shard_map/ppermute | solution.py:23
  12.4 40.1 %collective-permute-start.1 = (f32[4,1,512]{2,1,0:T(1,128)S(1)}, f32[4,1,512]{2,1,0:T(1,128)S(1)}, u32[]{:S(2)}, u32[]{:S(2)}) collective-permute-start(f32[4,1,512]{2,1,0:T(1,128)S(1)} %get-tuple-element.39), channel_id=1, source_target_pairs={{4,0},{8,4},{12,8},{16,12},{20,16},{24,20},{28,24},{32,28},{36,32}... | collective-permute-start | bytes 24584 | tf_op jit(solution)/shard_map/ppermute | solution.py:25
  59.8 91.5 %all-gather.19.cloned.1.call-start = ((), (), s32[]{:S(2)}) async-start(), calls=%async_computation.1 | async-start | bytes 3440640 | tf_op jit(solution)/shard_map/all_gather | solution.py:80
  60.7 40.3 %collective-permute-start.2 = (f32[4,1,512]{2,1,0:T(1,128)S(1)}, f32[4,1,512]{2,1,0:T(1,128)S(1)}, u32[]{:S(2)}, u32[]{:S(2)}) collective-permute-start(f32[4,1,512]{2,1,0:T(1,128)S(1)} %get-tuple-element.36), channel_id=1, source_target_pairs={{0,4},{4,8},{8,12},{12,16},{16,20},{20,24},{24,28},{28,32},{32,36}... | collective-permute-start | bytes 24584 | tf_op jit(solution)/shard_map/ppermute | solution.py:23
  62.0 39.0 %collective-permute-start.3 = (f32[4,1,512]{2,1,0:T(1,128)S(1)}, f32[4,1,512]{2,1,0:T(1,128)S(1)}, u32[]{:S(2)}, u32[]{:S(2)}) collective-permute-start(f32[4,1,512]{2,1,0:T(1,128)S(1)} %get-tuple-element.37), channel_id=1, source_target_pairs={{4,0},{8,4},{12,8},{16,12},{20,16},{24,20},{28,24},{32,28},{36,32}... | collective-permute-start | bytes 24584 | tf_op jit(solution)/shard_map/ppermute | solution.py:25
  108.7 95.0 %all-gather.21.cloned.1.call-start = ((), (), s32[]{:S(2)}) async-start(), calls=%async_computation.2 | async-start | bytes 3440640 | tf_op jit(solution)/shard_map/all_gather | solution.py:80
  109.6 46.4 %collective-permute-start.4 = (f32[4,1,512]{2,1,0:T(1,128)S(1)}, f32[4,1,512]{2,1,0:T(1,128)S(1)}, u32[]{:S(2)}, u32[]{:S(2)}) collective-permute-start(f32[4,1,512]{2,1,0:T(1,128)S(1)} %get-tuple-element.34), channel_id=1, source_target_pairs={{0,4},{4,8},{8,12},{12,16},{16,20},{20,24},{24,28},{28,32},{32,36}... | collective-permute-start | bytes 24584 | tf_op jit(solution)/shard_map/ppermute | solution.py:23
  112.7 43.3 %collective-permute-start.5 = (f32[4,1,512]{2,1,0:T(1,128)S(1)}, f32[4,1,512]{2,1,0:T(1,128)S(1)}, u32[]{:S(2)}, u32[]{:S(2)}) collective-permute-start(f32[4,1,512]{2,1,0:T(1,128)S(1)} %get-tuple-element.35), channel_id=1, source_target_pairs={{4,0},{8,4},{12,8},{16,12},{20,16},{24,20},{28,24},{32,28},{36,32}... | collective-permute-start | bytes 24584 | tf_op jit(solution)/shard_map/ppermute | solution.py:25
  161.1 95.7 %all-gather.23.cloned.1.call-start = ((), (), s32[]{:S(2)}) async-start(), calls=%async_computation.3 | async-start | bytes 3440640 | tf_op jit(solution)/shard_map/all_gather | solution.py:80
  162.1 44.6 %collective-permute-start.6 = (f32[4,1,512]{2,1,0:T(1,128)S(1)}, f32[4,1,512]{2,1,0:T(1,128)S(1)}, u32[]{:S(2)}, u32[]{:S(2)}) collective-permute-start(f32[4,1,512]{2,1,0:T(1,128)S(1)} %get-tuple-element.32), channel_id=1, source_target_pairs={{0,4},{4,8},{8,12},{12,16},{16,20},{20,24},{24,28},{28,32},{32,36}... | collective-permute-start | bytes 24584 | tf_op jit(solution)/shard_map/ppermute | solution.py:23
  165.2 41.5 %collective-permute-start.7 = (f32[4,1,512]{2,1,0:T(1,128)S(1)}, f32[4,1,512]{2,1,0:T(1,128)S(1)}, u32[]{:S(2)}, u32[]{:S(2)}) collective-permute-start(f32[4,1,512]{2,1,0:T(1,128)S(1)} %get-tuple-element.33), channel_id=1, source_target_pairs={{4,0},{8,4},{12,8},{16,12},{20,16},{24,20},{28,24},{32,28},{36,32}... | collective-permute-start | bytes 24584 | tf_op jit(solution)/shard_map/ppermute | solution.py:25
  214.2 94.9 %all-gather.25.cloned.1.call-start = ((), (), s32[]{:S(2)}) async-start(), calls=%async_computation.4 | async-start | bytes 3440640 | tf_op jit(solution)/shard_map/all_gather | solution.py:80
  215.2 46.2 %collective-permute-start.8 = (f32[4,1,512]{2,1,0:T(1,128)S(1)}, f32[4,1,512]{2,1,0:T(1,128)S(1)}, u32[]{:S(2)}, u32[]{:S(2)}) collective-permute-start(f32[4,1,512]{2,1,0:T(1,128)S(1)} %get-tuple-element.30), channel_id=1, source_target_pairs={{0,4},{4,8},{8,12},{12,16},{16,20},{20,24},{24,28},{28,32},{32,36}... | collective-permute-start | bytes 24584 | tf_op jit(solution)/shard_map/ppermute | solution.py:23
  218.3 43.1 %collective-permute-start.9 = (f32[4,1,512]{2,1,0:T(1,128)S(1)}, f32[4,1,512]{2,1,0:T(1,128)S(1)}, u32[]{:S(2)}, u32[]{:S(2)}) collective-permute-start(f32[4,1,512]{2,1,0:T(1,128)S(1)} %get-tuple-element.31), channel_id=1, source_target_pairs={{4,0},{8,4},{12,8},{16,12},{20,16},{24,20},{28,24},{32,28},{36,32}... | collective-permute-start | bytes 24584 | tf_op jit(solution)/shard_map/ppermute | solution.py:25
  266.5 95.3 %all-gather.27.cloned.1.call-start = ((), (), s32[]{:S(2)}) async-start(), calls=%async_computation.5 | async-start | bytes 3440640 | tf_op jit(solution)/shard_map/all_gather | solution.py:80
  267.4 44.7 %collective-permute-start.10 = (f32[4,1,512]{2,1,0:T(1,128)S(1)}, f32[4,1,512]{2,1,0:T(1,128)S(1)}, u32[]{:S(2)}, u32[]{:S(2)}) collective-permute-start(f32[4,1,512]{2,1,0:T(1,128)S(1)} %get-tuple-element.28), channel_id=1, source_target_pairs={{0,4},{4,8},{8,12},{12,16},{16,20},{20,24},{24,28},{28,32},{32,36}... | collective-permute-start | bytes 24584 | tf_op jit(solution)/shard_map/ppermute | solution.py:23
  270.6 41.5 %collective-permute-start.11 = (f32[4,1,512]{2,1,0:T(1,128)S(1)}, f32[4,1,512]{2,1,0:T(1,128)S(1)}, u32[]{:S(2)}, u32[]{:S(2)}) collective-permute-start(f32[4,1,512]{2,1,0:T(1,128)S(1)} %get-tuple-element.29), channel_id=1, source_target_pairs={{4,0},{8,4},{12,8},{16,12},{20,16},{24,20},{28,24},{32,28},{36,32}... | collective-permute-start | bytes 24584 | tf_op jit(solution)/shard_map/ppermute | solution.py:25
  319.0 93.3 %all-gather.29.cloned.1.call-start = ((), (), s32[]{:S(2)}) async-start(), calls=%async_computation.6 | async-start | bytes 3440640 | tf_op jit(solution)/shard_map/all_gather | solution.py:80
  319.1 45.7 %collective-permute-start.12 = (f32[4,1,512]{2,1,0:T(1,128)S(1)}, f32[4,1,512]{2,1,0:T(1,128)S(1)}, u32[]{:S(2)}, u32[]{:S(2)}) collective-permute-start(f32[4,1,512]{2,1,0:T(1,128)S(1)} %get-tuple-element.26), channel_id=1, source_target_pairs={{0,4},{4,8},{8,12},{12,16},{16,20},{20,24},{24,28},{28,32},{32,36}... | collective-permute-start | bytes 24584 | tf_op jit(solution)/shard_map/ppermute | solution.py:23
  322.2 42.5 %collective-permute-start.13 = (f32[4,1,512]{2,1,0:T(1,128)S(1)}, f32[4,1,512]{2,1,0:T(1,128)S(1)}, u32[]{:S(2)}, u32[]{:S(2)}) collective-permute-start(f32[4,1,512]{2,1,0:T(1,128)S(1)} %get-tuple-element.27), channel_id=1, source_target_pairs={{4,0},{8,4},{12,8},{16,12},{20,16},{24,20},{28,24},{32,28},{36,32}... | collective-permute-start | bytes 24584 | tf_op jit(solution)/shard_map/ppermute | solution.py:25
  370.5 95.6 %all-gather.31.cloned.1.call-start = ((), (), s32[]{:S(2)}) async-start(), calls=%async_computation.7 | async-start | bytes 3440640 | tf_op jit(solution)/shard_map/all_gather | solution.py:80
  371.5 45.7 %collective-permute-start.14 = (f32[4,1,512]{2,1,0:T(1,128)S(1)}, f32[4,1,512]{2,1,0:T(1,128)S(1)}, u32[]{:S(2)}, u32[]{:S(2)}) collective-permute-start(f32[4,1,512]{2,1,0:T(1,128)S(1)} %get-tuple-element.24), channel_id=1, source_target_pairs={{0,4},{4,8},{8,12},{12,16},{16,20},{20,24},{24,28},{28,32},{32,36}... | collective-permute-start | bytes 24584 | tf_op jit(solution)/shard_map/ppermute | solution.py:23
  374.6 42.6 %collective-permute-start.15 = (f32[4,1,512]{2,1,0:T(1,128)S(1)}, f32[4,1,512]{2,1,0:T(1,128)S(1)}, u32[]{:S(2)}, u32[]{:S(2)}) collective-permute-start(f32[4,1,512]{2,1,0:T(1,128)S(1)} %get-tuple-element.25), channel_id=1, source_target_pairs={{4,0},{8,4},{12,8},{16,12},{20,16},{24,20},{28,24},{32,28},{36,32}... | collective-permute-start | bytes 24584 | tf_op jit(solution)/shard_map/ppermute | solution.py:25
  (34 other events, 394.8 us)
Sparse Core Ops, SparseCore 0:
  59.9 38.9 all-gather.16
  108.8 42.4 all-gather.18
  161.2 42.4 all-gather.20
  214.4 42.4 all-gather.22
  266.6 42.4 all-gather.24
  319.1 42.6 all-gather.26
  370.7 41.6 all-gather.28
  421.6 35.3 all-gather.30
